TPU v7x, 32 devices: a whole 2x2x4 slice. The times are simulated.
32 devices in a mesh: col: 2 (over core), dp: 16 (over z, y, x).
Axes of the slice: x: 2, y: 2, z: 4, core: 2. Of those that a mesh axis runs over, the one named last changes fastest.
Arguments:
- acts: bfloat16 [6144, 5120], P('dp', 'col'), may hold values from -6 to 6
- out_grad: bfloat16 [6144, 8192], P('dp', 'col'), may hold values from -6 to 6
- projection: bfloat16 [5120, 256], replicated, may hold values from -0.078125 to 0.078125
- weight: bfloat16 [5120, 8192], P('dp', 'col'), may hold values from -0.078125 to 0.078125
- m_codes: int32 [256, 8192], P('dp', 'col'), may hold values from -127 to 127
- m_exps: int32 [256, 256], P('dp', 'col'), may hold values from -16 to -9
- v_codes: int32 [256, 8192], P('dp', 'col'), may hold values from 1 to 127
- v_exps: int32 [256, 256], P('dp', 'col'), may hold values from -24 to -18
- next_acts: bfloat16 [6144, 5120], P('dp', 'col'), may hold values from -6 to 6
Outputs:
- next_out: bfloat16 [6144, 8192], P('dp', 'col')
- new_weight: bfloat16 [5120, 8192], P('dp', 'col')
- update: float32 [256, 8192], P('dp', 'col')
Inputs may be any that keep to these rules, and one draw needn't show every extreme that they name: `v_codes`: second moment mantissas are positive.
All inputs are finite; a program needn't handle non-finite values.
Results may differ from a plain program's by a relative error of at most 0.0051.
Values may be sent and summed in bfloat16 or wider, within the bound.
A program may use at most 128 MiB of HBM per device.

v0:
```python
import jax
import jax.numpy as jnp
from jax import lax
from jax.sharding import PartitionSpec as P

learn_rate = 0.02
beta_one = 0.9
beta_two = 0.999
epsilon = 1e-08
correct_first = 0.9999734386011124
correct_second = 0.0952078528862904


def decode(codes, exps):
    scale = jnp.exp2(exps.astype(jnp.float32))
    rows = codes.shape[0]
    values = (codes.astype(jnp.float32) / 128.0).reshape(
        rows, exps.shape[1], codes.shape[1] // exps.shape[1]
    )
    return (values * scale[:, :, None]).reshape(rows, codes.shape[1])


def body(acts, out_grad, projection, weight, m_codes, m_exps, v_codes, v_exps, next_acts):
    col_width = acts.shape[1]
    col_start = lax.axis_index("col") * col_width
    proj_cols = lax.dynamic_slice_in_dim(projection, col_start, col_width, 0)
    partial_value = jnp.dot(acts, proj_cols, preferred_element_type=jnp.float32)
    lowrank = lax.psum(partial_value, "col").astype(jnp.bfloat16)
    tokens_all = acts.shape[0] * lax.axis_size("dp")
    grad = (
        lax.psum_scatter(
            lax.dot_general(
                lowrank, out_grad, (((0,), (0,)), ((), ())), preferred_element_type=jnp.float32
            ),
            "dp",
            scatter_dimension=0,
            tiled=True,
        )
        / tokens_all
    )
    m_old = decode(m_codes, m_exps)
    v_old = decode(v_codes, v_exps)
    first = beta_one * m_old + (1.0 - beta_one) * grad
    second = beta_two * v_old + (1.0 - beta_two) * grad * grad
    update = first / correct_first / (jnp.sqrt(second / correct_second) + epsilon)
    direction = update.astype(jnp.bfloat16)
    full_next = lax.all_gather(next_acts, "col", axis=1, tiled=True)
    row_count = weight.shape[0]
    row_start = lax.axis_index("dp") * row_count
    proj_rows = lax.dynamic_slice_in_dim(projection, row_start, row_count, 0)
    part = proj_rows
    delta = jnp.dot(
        part,
        lax.all_gather(direction, "dp", axis=0, tiled=True),
        preferred_element_type=jnp.float32,
    )
    new_weight = (weight.astype(jnp.float32) - learn_rate * delta).astype(jnp.bfloat16)
    part = full_next
    result = jnp.dot(
        part,
        lax.all_gather(new_weight, "dp", axis=0, tiled=True),
        preferred_element_type=jnp.float32,
    )
    return (result.astype(jnp.bfloat16), new_weight, update)


def solution(mesh):
    placed = (
        P("dp", "col"),
        P("dp", "col"),
        P(),
        P("dp", "col"),
        P("dp", "col"),
        P("dp", "col"),
        P("dp", "col"),
        P("dp", "col"),
        P("dp", "col"),
    )
    return jax.shard_map(
        body,
        mesh=mesh,
        in_specs=placed,
        out_specs=(P("dp", "col"), P("dp", "col"), P("dp", "col")),
        check_vma=False,
    )
```

profile of v0, /device:TPU:0, one launch (start us, length us, event | category | flops | bytes accessed | tf_op | source)
XLA Modules:
  0.0 668.8 jit_solution(5386757203019559583)
XLA Ops:
  7.2 0.0 reduce-scatter.2.cloned.1.call-start
  7.2 3.0 fusion.5
  10.2 5.3 all-reduce.1
  15.5 4.1 fusion.14
  19.7 0.0 reduce-scatter.2.cloned.1.call-update
  19.7 0.0 all-gather.4.cloned.1.call-start
  19.7 0.6 copy-done.4
  20.4 0.3 mul.70
  20.7 0.5 mul.71
  21.2 1.3 mul.62
  22.5 1.7 mul.63
  24.2 93.1 %reduce-scatter.2.cloned.1.call-done = f32[16,4096]{1,0:T(8,128)} async-done(((f32[256,4096]{1,0:T(8,128)}), f32[16,4096]{1,0:T(8,128)}) %reduce-scatter.2.cloned.1.call-update) | async-done | bytes 262160 | tf_op jit(solution)/shard_map/reduce_scatter | solution.py:31
  117.4 2.0 fusion.13
  119.4 0.0 all-gather.4.cloned.1.call-update
  119.4 0.0 all-gather.8.cloned.1.call-start
  119.4 0.7 all-gather.8.cloned.1.call-update
  120.1 0.0 all-gather.6.cloned.1.call-start
  120.2 60.9 %all-gather.4.cloned.1.call-done = bf16[256,4096]{1,0:T(8,128)(2,1)} async-done(((bf16[16,4096]{1,0:T(8,128)(2,1)}), bf16[256,4096]{1,0:T(8,128)(2,1)}) %all-gather.4.cloned.1.call-update) | async-done | bytes 2097168 | tf_op jit(solution)/shard_map/all_gather | solution.py:54
  181.1 4.1 fusion.1
  185.1 0.0 all-gather.6.cloned.1.call-update
  185.1 9.4 %all-gather.8.cloned.1.call-done = bf16[384,5120]{1,0:T(8,128)(2,1)} async-done(((bf16[384,2560]{1,0:T(8,128)(2,1)}), bf16[384,5120]{1,0:T(8,128)(2,1)}) %all-gather.8.cloned.1.call-update) | async-done | bytes 3932176 | tf_op jit(solution)/shard_map/all_gather | solution.py:47
  194.6 434.4 %all-gather.6.cloned.1.call-done = bf16[5120,4096]{1,0:T(8,128)(2,1)} async-done(((bf16[320,4096]{1,0:T(8,128)(2,1)}), bf16[5120,4096]{1,0:T(8,128)(2,1)}) %all-gather.6.cloned.1.call-update) | async-done | bytes 41943056 | tf_op jit(solution)/shard_map/all_gather | solution.py:61
  628.9 28.7 %fusion.2 = bf16[384,4096]{0,1:T(8,128)(2,1)} fusion(bf16[5120,4096]{1,0:T(8,128)(2,1)} %all-gather.6.cloned.1.call-done, bf16[384,5120]{1,0:T(8,128)(2,1)} %all-gather.8.cloned.1.call-done), kind=kOutput, calls=%fused_computation.4 | convolution fusion | flops 16107700224 | bytes 49020928 | tf_op jit(solution)/shard_map/dot_general | solution.py:59
  657.6 4.6 copy.13
  (13 shorter events, 0.0 us)
Async XLA Ops:
  7.2 8.4 %copy-start = (bf16[384,4096]{1,0:T(8,128)(2,1)S(1)}, bf16[384,4096]{1,0:T(8,128)(2,1)}, u32[]{:S(2)}) copy-start(bf16[384,4096]{1,0:T(8,128)(2,1)} %param.10) | copy-start | bytes 9437188
  7.2 110.2 %reduce-scatter.2.cloned.1.call-start = ((), (), s32[]{:S(2)}) async-start(), calls=%async_computation.1 | async-start | bytes 4456448 | tf_op jit(solution)/shard_map/reduce_scatter | solution.py:31
  19.7 0.7 copy-start.4
  19.7 1.5 copy-start.5
  19.7 97.7 %copy-start.3 = (s32[16,4096]{1,0:T(8,128)S(1)}, s32[16,4096]{1,0:T(8,128)}, u32[]{:S(2)}) copy-start(s32[16,4096]{1,0:T(8,128)} %param.15) | copy-start | bytes 786436
  19.7 161.4 %all-gather.4.cloned.1.call-start = ((), (), s32[]{:S(2)}) async-start(), calls=%async_computation.2 | async-start | bytes 2228224 | tf_op jit(solution)/shard_map/all_gather | solution.py:54
  21.2 159.9 %copy-start.2 = (bf16[320,4096]{1,0:T(8,128)(2,1)S(1)}, bf16[320,4096]{1,0:T(8,128)(2,1)}, u32[]{:S(2)}) copy-start(bf16[320,4096]{1,0:T(8,128)(2,1)} %param.12) | copy-start | bytes 7864324
  119.4 75.2 %all-gather.8.cloned.1.call-start = ((), (), s32[]{:S(2)}) async-start(), calls=%async_computation.4 | async-start | bytes 5898240 | tf_op jit(solution)/shard_map/all_gather | solution.py:47
  120.1 508.8 %all-gather.6.cloned.1.call-start = ((), (), s32[]{:S(2)}) async-start(), calls=%async_computation.3 | async-start | bytes 44564480 | tf_op jit(solution)/shard_map/all_gather | solution.py:61
  628.9 33.3 %copy-start.1 = (bf16[384,4096]{1,0:T(8,128)(2,1)S(1)}, bf16[384,4096]{1,0:T(8,128)(2,1)}, u32[]{:S(2)}) copy-start(bf16[384,4096]{1,0:T(8,128)(2,1)} %param.10) | copy-start | bytes 9437188
Sparse Core Ops, SparseCore 0:
  19.8 97.5 reduce-scatter.1
  120.7 60.3 all-gather.3
  182.6 11.9 all-gather.7
  197.7 431.2 all-gather.5
where the time goes:
time: 669 us
  waiting for transfers between devices  599 us (90%)
  matrix products  39.8 us (6%)
  between operations  13.8 us (2%)
  local copies, waits for them, and re-layouts  9.11 us (1%)
    all_gather x1, waiting for transfers between devices, body(): lax.all_gather(new_weight, 'dp', axis=0, tiled=True)  434 us
    reduce_scatter x1, waiting for transfers between devices, body(): lax.psum_scatter(lax.dot_general(lowrank, out_grad, (((0,), (0,)), ((), (...  93.1 us
    all_gather x1, waiting for transfers between devices, body(): lax.all_gather(direction, 'dp', axis=0, tiled=True)  60.9 us
    dot_general x1, matrix products, body(): jnp.dot(part, lax.all_gather(new_weight, 'dp', axis=0, tiled=True), prefe...  28.7 us
  transfers between devices with their start and end apart: 4, of which 4 were waited for; matrix products, arithmetic and copies ran while one was open for 1% of the time, Pallas kernels for 0%

commit v1 on v0

--- a/solution.py
+++ b/solution.py
@@ -1,6 +1,10 @@
+import functools
+
 import jax
 import jax.numpy as jnp
 from jax import lax
+from jax.experimental import pallas as pl
+from jax.experimental.pallas import tpu as pltpu
 from jax.sharding import PartitionSpec as P
 
 learn_rate = 0.02
@@ -9,6 +13,401 @@
 epsilon = 1e-08
 correct_first = 0.9999734386011124
 correct_second = 0.0952078528862904
+MESH = pl.DeviceIdType.MESH
+SIDE = 4
+SPLITS = 4
+BF = jnp.bfloat16
+F32 = jnp.float32
+
+
+def dot(a, b):
+    return jnp.dot(a, b, preferred_element_type=F32)
+
+
+def kernel(
+    layers, tokens_all,
+    acts, grads, proj, weight, mc, me, vc, ve, nxt,
+    out, new_weight, update,
+    acts_v, proj_v, grads_v, weight_v, mc_v, me_v, vc_v, ve_v,
+    low_v, low_t, gpart, grecv, gz, gsum, dirs, upd_v, nw_v,
+    a_v, b_v, n_v, c_v,
+    load_sem, low_send, low_recv, g_send, g_recv, gz_send, gz_recv,
+    dz_send, dz_recv, di_send, di_recv, a_send, a_fwd, a_recv,
+    bi_send, bz_send, b_recv, c_send, c_recv, c_loc, out_sem,
+):
+    c = lax.axis_index("col")
+    dp = lax.axis_index("dp")
+    z = dp // SIDE
+    q = dp % SIDE
+    rows, width = weight.shape
+    block = width // SIDE
+    part = block // SPLITS
+    tok, half = nxt.shape
+    rank = proj.shape[1]
+    rstep = mc.shape[0]
+
+    def peer(j):
+        return ((q // 2 + j // 2) % 2) * 2 + (q % 2 + j % 2) % 2
+
+    def at(zz, qq):
+        return (c, zz * SIDE + qq)
+
+    def remote(src, dst, ss, rs, dev):
+        return pltpu.make_async_remote_copy(
+            src_ref=src, dst_ref=dst, send_sem=ss, recv_sem=rs,
+            device_id=dev, device_id_type=MESH,
+        )
+
+    other = (1 - c, dp)
+
+    def loop(n, body, first=0):
+        def step(i, carry):
+            body(i)
+            return carry
+        lax.fori_loop(first, n, step, 0)
+
+    loads = [
+        (acts, acts_v), (proj, proj_v), (grads, grads_v), (weight, weight_v),
+        (mc, mc_v), (me, me_v), (vc, vc_v), (ve, ve_v), (nxt, a_v.at[q, c]),
+    ]
+    loads = [pltpu.make_async_copy(s, d, load_sem.at[i]) for i, (s, d) in enumerate(loads)]
+    for copy in loads:
+        copy.start()
+
+    barrier = pltpu.get_barrier_semaphore()
+    partners = [other] + [at(z, peer(j)) for j in range(1, SIDE)]
+    partners += [at((z + o) % layers, q) for o in range(1, layers)]
+    for dev in partners:
+        pl.semaphore_signal(barrier, inc=1, device_id=dev, device_id_type=MESH)
+    pl.semaphore_wait(barrier, len(partners))
+
+    def cols(qq, s):
+        return pl.ds(pl.multiple_of(qq * block + s * part, 128), part)
+
+    def b_in(s, j):
+        return remote(weight.at[:, cols(peer(j), s)], b_v.at[s, dp],
+                      bi_send.at[s, j], b_recv.at[s, dp], at(z, peer(j)))
+
+    def b_own(s):
+        return pltpu.make_async_copy(weight.at[:, cols(q, s)], b_v.at[s, dp], bi_send.at[s, 0])
+
+    def b_z(s, dpi, way, own=False):
+        src = weight.at[:, cols(q, s)] if own else b_v.at[s, dpi]
+        return remote(src, b_v.at[s, dpi], bz_send.at[way, s, dpi], b_recv.at[s, dpi],
+                      at((z + (1 if way == 0 else layers - 1)) % layers, q))
+
+    def b_send_z(s, dpi, way, own=False):
+        @pl.when((z < layers - 1) if way == 0 else (z > 0))
+        def _():
+            b_z(s, dpi, way, own).start()
+
+    def b_wait(s, dpi):
+        remote(b_v.at[s, dpi], b_v.at[s, dpi], bi_send.at[s, 0], b_recv.at[s, dpi], other).wait_recv()
+
+    def send_in(s):
+        for j in range(1, SIDE):
+            b_in(s, j).start()
+        b_own(s).start()
+
+    def send_own(s):
+        for way in range(2):
+            b_send_z(s, dp, way, own=True)
+
+    def layer_stage(s):
+        def one(j):
+            dpi = z * SIDE + peer(j)
+            b_wait(s, dpi)
+            for way in range(2):
+                b_send_z(s, dpi, way)
+        loop(SIDE, one, 1)
+
+    def far_stage(s, d):
+        def one(j):
+            for way in range(2):
+                src = z - d if way == 0 else z + d
+
+                @pl.when((src >= 0) & (src < layers))
+                def _():
+                    dpi = src * SIDE + peer(j)
+                    b_wait(s, dpi)
+                    b_send_z(s, dpi, way)
+        loop(SIDE, one)
+
+    def low_copy():
+        return remote(low_v.at[0], low_v.at[1], low_send, low_recv, other)
+
+    def g_copy(j):
+        return remote(gpart.at[:, peer(j)], grecv.at[j], g_send.at[j], g_recv.at[j], at(z, peer(j)))
+
+    def gz_copy(o):
+        zz = (z + o) % layers
+        return remote(gsum.at[zz], gz.at[o], gz_send.at[o], gz_recv.at[o], at(zz, q))
+
+    def dz_copy(o):
+        return remote(dirs.at[z, q], dirs.at[z, q], dz_send.at[o], dz_recv.at[o], at((z + o) % layers, q))
+
+    def dz_wait(o):
+        zz = (z + layers - o) % layers
+        remote(dirs.at[zz, q], dirs.at[zz, q], dz_send.at[o], dz_recv.at[o], other).wait_recv()
+
+    def di_copy(j):
+        return remote(dirs.at[:, q], dirs.at[:, q], di_send.at[j], di_recv.at[j], at(z, peer(j)))
+
+    def di_wait(j):
+        remote(dirs.at[:, peer(j)], dirs.at[:, peer(j)], di_send.at[j], di_recv.at[j], other).wait_recv()
+
+    def a_copy(j):
+        return remote(nxt, a_v.at[q, c], a_send.at[j], a_recv.at[q, c], at(z, peer(j)))
+
+    def a_cross(j):
+        qq = peer(j)
+        src = nxt if j == 0 else a_v.at[qq, c]
+        return remote(src, a_v.at[qq, c], a_fwd.at[j], a_recv.at[qq, c], other)
+
+    def a_wait(qq, cc):
+        remote(a_v.at[qq, cc], a_v.at[qq, cc], a_send.at[0], a_recv.at[qq, cc], other).wait_recv()
+
+    wide = 512 if width % 512 == 0 else 128
+
+    def slab(i):
+        return pl.ds(pl.multiple_of(i * wide, 128), wide)
+
+    def gradient():
+        loads[0].wait()
+        loads[1].wait()
+        low_v[0] = dot(acts_v[...], proj_v[pl.ds(pl.multiple_of(c * half, 128), half), :])
+        low_copy().start()
+        loads[2].wait()
+        low_copy().wait_recv()
+        low_t[...] = jnp.transpose(low_v[0] + low_v[1]).astype(BF)
+
+        def one(i):
+            g = dot(low_t[...], grads_v[:, slab(i)])
+            gpart[:, :, :, slab(i)] = g.astype(BF).reshape(layers, SIDE, rstep, wide)
+        loop(width // wide, one)
+        for j in range(1, SIDE):
+            g_copy(j).start()
+
+    def gradient_layer():
+        for j in range(1, SIDE):
+            g_copy(j).wait_recv()
+
+        def one(i):
+            total = gpart[:, q, :, slab(i)].astype(F32)
+            for j in range(1, SIDE):
+                total += grecv[j, :, :, slab(i)].astype(F32)
+            gsum[:, :, slab(i)] = total.astype(BF)
+        loop(width // wide, one)
+        for o in range(1, layers):
+            gz_copy(o).start()
+
+    def adam():
+        for i in range(4, 8):
+            loads[i].wait()
+        for o in range(1, layers):
+            gz_copy(o).wait_recv()
+        blocks = me.shape[1]
+        each = width // blocks
+        m_scale = jnp.exp2(me_v[...].astype(F32)).astype(BF)
+        v_scale = jnp.exp2(ve_v[...].astype(F32)).astype(BF)
+
+        def one(i):
+            total = gsum[z, :, slab(i)].astype(F32)
+            for o in range(1, layers):
+                total += gz[o, :, slab(i)].astype(F32)
+            grad = total / tokens_all
+            owner = (lax.broadcasted_iota(jnp.int32, (blocks, wide), 1) + i * wide) // each
+            pick = (owner == lax.broadcasted_iota(jnp.int32, (blocks, wide), 0)).astype(F32).astype(BF)
+            m_old = mc_v[:, slab(i)].astype(F32) / 128.0 * dot(m_scale, pick)
+            v_old = vc_v[:, slab(i)].astype(F32) / 128.0 * dot(v_scale, pick)
+            first = beta_one * m_old + (1.0 - beta_one) * grad
+            second = beta_two * v_old + (1.0 - beta_two) * grad * grad
+            u = first / correct_first / (jnp.sqrt(second / correct_second) + epsilon)
+            upd_v[:, slab(i)] = u
+            dirs[z, q, :, slab(i)] = u.astype(BF)
+        loop(width // wide, one)
+        for o in range(1, layers):
+            dz_copy(o).start()
+        pltpu.make_async_copy(upd_v, update, out_sem.at[0]).start()
+
+    def direction_layer():
+        for o in range(1, layers):
+            dz_wait(o)
+        for j in range(1, SIDE):
+            di_copy(j).start()
+
+    def weights():
+        for j in range(1, SIDE):
+            di_wait(j)
+        loads[3].wait()
+
+        def one(i):
+            d = dirs[:, :, :, slab(i)].reshape(rank, wide)
+            delta = dot(proj_v[pl.ds(pl.multiple_of(dp * rows, 16), rows), :], d)
+            nw_v[:, slab(i)] = (weight_v[:, slab(i)].astype(F32) - learn_rate * delta).astype(BF)
+        loop(width // wide, one)
+        pltpu.make_async_copy(nw_v, new_weight, out_sem.at[1]).start()
+
+    def tokens():
+        for j in range(1, SIDE):
+            a_wait(peer(j), c)
+            a_cross(j).start()
+        loads[8].wait()
+        for j in range(SIDE):
+            a_wait(peer(j), 1 - c)
+
+        def one(m):
+            n = dot(a_v[m, 0], proj_v[:half, :]) + dot(a_v[m, 1], proj_v[half:, :])
+            n_v[m] = (-learn_rate * n).astype(BF)
+        loop(SIDE, one)
+
+    def c_copy(s, m):
+        return remote(c_v.at[s, m], out.at[:, cols(q, s)], c_send.at[s, m], c_recv.at[s, q], at(z, m))
+
+    def c_local(s):
+        return pltpu.make_async_copy(c_v.at[s, q], out.at[:, cols(q, s)], c_loc.at[s])
+
+    per = half // rows
+
+    def product(s):
+        b_own(s).wait()
+
+        def one(j):
+            m = peer((j + 1) % SIDE)
+            d = dirs[:, :, :, cols(q, s)].reshape(rank, part)
+            r = dot(n_v[m], d)
+            for cc in range(2):
+                r += dot(a_v[m, cc], b_v[s, cc * per:(cc + 1) * per].reshape(half, part))
+            c_v[s, m] = r.astype(BF)
+
+            @pl.when(m != q)
+            def _():
+                c_copy(s, m).start()
+
+            @pl.when(m == q)
+            def _():
+                c_local(s).start()
+        loop(SIDE, one)
+
+    send_own(0)
+    send_in(0)
+    gradient()
+    for j in range(1, SIDE):
+        a_copy(j).start()
+    a_cross(0).start()
+    for s in range(1, SPLITS):
+        send_in(s)
+    extra = [gradient_layer, adam, direction_layer, weights, tokens]
+    events = []
+    for s in range(SPLITS):
+        events.append((layers * s - s - 1.5, s, 0))
+        for d in range(1, layers):
+            events.append((layers * s - s + d, s, d))
+    ready = []
+    for _, s, d in sorted(events):
+        if d == 0:
+            if s:
+                send_own(s)
+            layer_stage(s)
+        else:
+            far_stage(s, d)
+        if d == layers - 1:
+            ready.append(s)
+        if extra:
+            extra.pop(0)()
+        if not extra:
+            for t in ready:
+                product(t)
+            ready = []
+    while extra:
+        extra.pop(0)()
+    for t in ready:
+        product(t)
+
+    low_copy().wait_send()
+    for j in range(1, SIDE):
+        g_copy(j).wait_send()
+        di_copy(j).wait_send()
+        a_copy(j).wait_send()
+    for j in range(SIDE):
+        a_cross(j).wait_send()
+    for o in range(1, layers):
+        gz_copy(o).wait_send()
+        dz_copy(o).wait_send()
+    for s in range(SPLITS):
+        for j in range(1, SIDE):
+            b_in(s, j).wait_send()
+
+        def sent(dpi):
+            src = dpi // SIDE
+
+            @pl.when((src <= z) & (z < layers - 1))
+            def _():
+                b_z(s, dpi, 0).wait_send()
+
+            @pl.when((src >= z) & (z > 0))
+            def _():
+                b_z(s, dpi, 1).wait_send()
+        loop(layers * SIDE, sent)
+    pltpu.make_async_copy(upd_v, update, out_sem.at[0]).wait()
+    pltpu.make_async_copy(nw_v, new_weight, out_sem.at[1]).wait()
+
+    def done(j):
+        qq = peer(j)
+        for s in range(SPLITS):
+            remote(c_v.at[s, 0], out.at[:, cols(qq, s)], c_send.at[s, 0], c_recv.at[s, qq], other).wait_recv()
+            c_copy(s, qq).wait_send()
+    loop(SIDE, done, 1)
+    for s in range(SPLITS):
+        c_local(s).wait()
+
+
+def fused(acts, out_grad, projection, weight, m_codes, m_exps, v_codes, v_exps, next_acts):
+    dp = lax.axis_size("dp")
+    layers = dp // SIDE
+    rows, width = weight.shape
+    part = width // SIDE // SPLITS
+    tok, half = next_acts.shape
+    rank = projection.shape[1]
+    rstep = rank // dp
+    dma = lambda *s: pltpu.SemaphoreType.DMA(s)
+    any_spec = pl.BlockSpec(memory_space=pl.ANY)
+    like = lambda x: pltpu.VMEM(x.shape, x.dtype)
+    return pl.pallas_call(
+        functools.partial(kernel, layers, acts.shape[0] * dp),
+        out_shape=(
+            jax.ShapeDtypeStruct((tok, width), BF),
+            jax.ShapeDtypeStruct((rows, width), BF),
+            jax.ShapeDtypeStruct((rstep, width), F32),
+        ),
+        in_specs=[any_spec] * 9,
+        out_specs=(any_spec,) * 3,
+        scratch_shapes=[
+            like(acts), like(projection), like(out_grad), like(weight),
+            like(m_codes), like(m_exps), like(v_codes), like(v_exps),
+            pltpu.VMEM((2, acts.shape[0], rank), F32),
+            pltpu.VMEM((rank, acts.shape[0]), BF),
+            pltpu.VMEM((layers, SIDE, rstep, width), BF),
+            pltpu.VMEM((SIDE, layers, rstep, width), BF),
+            pltpu.VMEM((layers, rstep, width), BF),
+            pltpu.VMEM((layers, rstep, width), BF),
+            pltpu.VMEM((layers, SIDE, rstep, width), BF),
+            pltpu.VMEM((rstep, width), F32),
+            pltpu.VMEM((rows, width), BF),
+            pltpu.VMEM((SIDE, 2, tok, half), BF),
+            pltpu.VMEM((SPLITS, dp, rows, part), BF),
+            pltpu.VMEM((SIDE, tok, rank), BF),
+            pltpu.VMEM((SPLITS, SIDE, tok, part), BF),
+            dma(9), pltpu.SemaphoreType.DMA, pltpu.SemaphoreType.DMA, dma(SIDE), dma(SIDE),
+            dma(layers), dma(layers),
+            dma(layers), dma(layers), dma(SIDE), dma(SIDE), dma(SIDE), dma(SIDE), dma(SIDE, 2),
+            dma(SPLITS, SIDE), dma(2, SPLITS, dp), dma(SPLITS, dp),
+            dma(SPLITS, SIDE), dma(SPLITS, SIDE), dma(SPLITS), dma(2),
+        ],
+        compiler_params=pltpu.CompilerParams(
+            collective_id=0, has_side_effects=True, vmem_limit_bytes=60 * 2**20
+        ),
+    )(acts, out_grad, projection, weight, m_codes, m_exps, v_codes, v_exps, next_acts)
 
 
 def decode(codes, exps):
@@ -20,7 +419,26 @@
     return (values * scale[:, :, None]).reshape(rows, codes.shape[1])
 
 
+def fits(acts, out_grad, projection, weight, m_codes, m_exps, v_codes, v_exps, next_acts):
+    dp = lax.axis_size("dp")
+    rank = projection.shape[1]
+    return (
+        lax.axis_size("col") == 2
+        and dp % (2 * SIDE) == 0
+        and rank % (16 * dp) == 0
+        and weight.shape[0] % 16 == 0
+        and weight.shape[1] % (SIDE * SPLITS * 128) == 0
+        and next_acts.shape[0] % 16 == 0
+        and next_acts.shape[1] % 128 == 0
+        and acts.shape[0] % 16 == 0
+        and next_acts.shape[1] % weight.shape[0] == 0
+    )
+
+
 def body(acts, out_grad, projection, weight, m_codes, m_exps, v_codes, v_exps, next_acts):
+    given = (acts, out_grad, projection, weight, m_codes, m_exps, v_codes, v_exps, next_acts)
+    if fits(*given):
+        return fused(*given)
     col_width = acts.shape[1]
     col_start = lax.axis_index("col") * col_width
     proj_cols = lax.dynamic_slice_in_dim(projection, col_start, col_width, 0)
@@ -49,17 +467,16 @@
     row_start = lax.axis_index("dp") * row_count
     proj_rows = lax.dynamic_slice_in_dim(projection, row_start, row_count, 0)
     part = proj_rows
-    delta = jnp.dot(
-        part,
-        lax.all_gather(direction, "dp", axis=0, tiled=True),
-        preferred_element_type=jnp.float32,
-    )
+    direction_all = lax.all_gather(direction, "dp", axis=0, tiled=True)
+    delta = jnp.dot(part, direction_all, preferred_element_type=jnp.float32)
     new_weight = (weight.astype(jnp.float32) - learn_rate * delta).astype(jnp.bfloat16)
-    part = full_next
-    result = jnp.dot(
-        part,
-        lax.all_gather(new_weight, "dp", axis=0, tiled=True),
-        preferred_element_type=jnp.float32,
+    weight_all = lax.all_gather(weight, "dp", axis=0, tiled=True)
+    main = jnp.dot(full_next, weight_all, preferred_element_type=jnp.float32)
+    low_next = jnp.dot(full_next, projection, preferred_element_type=jnp.float32).astype(
+        jnp.bfloat16
+    )
+    result = main - learn_rate * jnp.dot(
+        low_next, direction_all, preferred_element_type=jnp.float32
     )
     return (result.astype(jnp.bfloat16), new_weight, update)
 

time: 669 us -> 322 us (0.48)
  waiting for transfers between devices: 599 us -> 0 us
  Pallas kernels: 0 us -> 315 us
  matrix products: 39.8 us -> 0 us
  between operations: 13.8 us -> 0.65 us
    all_gather x3 -> x0, waiting for transfers between devices: 505 us -> none  [the longest x1 434 us: body(): lax.all_gather(new_weight, 'dp', axis=0, tiled=True)]
    pallas_call x0 -> x1, Pallas kernels: none -> 315 us  [fused(): pl.pallas_call(functools.partial(kernel, layers, acts.shape[0] * dp), out...]
    reduce_scatter x1 -> x0, waiting for transfers between devices: 93.1 us -> none  [body(): lax.psum_scatter(lax.dot_general(lowrank, out_grad, (((0,), (0,)), ((), (...]
    dot_general x4 -> x0, matrix products: 39.8 us -> none  [the longest x1 28.7 us: body(): jnp.dot(part, lax.all_gather(new_weight, 'dp', axis=0, tiled=True), prefe...]
  transfers between devices with their start and end apart: 4 -> 0, of which waited for: 4 -> 0; matrix products, arithmetic and copies ran while one was open for 1% -> 0% of each run, Pallas kernels for 0% -> 0%
where the time goes in v1:
time: 322 us
  Pallas kernels  315 us (98%)
  local copies, waits for them, and re-layouts  6.26 us (2%)
    pallas_call x1, Pallas kernels, fused(): pl.pallas_call(functools.partial(kernel, layers, acts.shape[0] * dp), out...  315 us

profile of v1, /device:TPU:0, one launch (start us, length us, event | category | flops | bytes accessed | tf_op | source)
XLA Modules:
  0.0 322.2 jit_solution(2459143766235846805)
XLA Ops:
  0.6 315.3 %shard_map.112 = (bf16[384,4096]{1,0:T(8,128)(2,1)}, bf16[320,4096]{1,0:T(8,128)(2,1)}, f32[16,4096]{1,0:T(8,128)}) custom-call(bf16[384,2560]{1,0:T(8,128)(2,1)} %acts.1, bf16[384,4096]{1,0:T(8,128)(2,1)} %grads.1, bf16[5120,256]{1,0:T(8,128)(2,1)} %proj.1, bf16[320,4096]{1,0:T(8,128)(2,1)} %weight.1, s32[16,4096]{1,0:T(8,128)} %mc.1, s32[16,128]{1,0:T(8,128)} %me.1, ...), custom_call_target="tpu_custom_call" | custom-call | tf_op jit(solution)/shard_map/pallas_call | solution.py:376
  315.9 0.0 copy-start
  315.9 4.1 %copy.15 = bf16[384,4096]{1,0:T(8,128)(2,1)} copy(bf16[384,4096]{1,0:T(8,128)(2,1)} %get-tuple-element.6) | data formatting | bytes 6291456
  320.0 0.0 copy-done
  320.0 0.0 copy-start.1
  320.0 1.5 copy.16
  321.5 0.0 copy-done.1
  321.5 0.7 copy.17
Async XLA Ops:
  315.9 4.1 %copy-start = (bf16[320,4096]{1,0:T(8,128)(2,1)S(1)}, bf16[320,4096]{1,0:T(8,128)(2,1)}, u32[]{:S(2)}) copy-start(bf16[320,4096]{1,0:T(8,128)(2,1)} %get-tuple-element.7) | copy-start | bytes 7864324
  320.0 1.5 copy-start.1

commit v2 on v1

--- a/solution.py
+++ b/solution.py
@@ -15,7 +15,11 @@
 correct_second = 0.0952078528862904
 MESH = pl.DeviceIdType.MESH
 SIDE = 4
-SPLITS = 4
+SHARES = (3, 2, 2, 1)
+SPLITS = len(SHARES)
+UNITS = sum(SHARES)
+PLACES = (2, 4, 7, 4, 7, 9, 10)
+EARLY = 1
 BF = jnp.bfloat16
 F32 = jnp.float32
 
@@ -30,9 +34,9 @@
     out, new_weight, update,
     acts_v, proj_v, grads_v, weight_v, mc_v, me_v, vc_v, ve_v,
     low_v, low_t, gpart, grecv, gz, gsum, dirs, upd_v, nw_v,
-    a_v, b_v, n_v, c_v,
+    a_v, b_v, n_v, c_v, acc_v,
     load_sem, low_send, low_recv, g_send, g_recv, gz_send, gz_recv,
-    dz_send, dz_recv, di_send, di_recv, a_send, a_fwd, a_recv,
+    dz_send, dz_recv, di_send, di_recv, a_send, a_fwd, a_recv, ar_send, ar_recv,
     bi_send, bz_send, b_recv, c_send, c_recv, c_loc, out_sem,
 ):
     c = lax.axis_index("col")
@@ -41,7 +45,8 @@
     q = dp % SIDE
     rows, width = weight.shape
     block = width // SIDE
-    part = block // SPLITS
+    unit = block // UNITS
+    parts = [unit * k for k in SHARES]
     tok, half = nxt.shape
     rank = proj.shape[1]
     rstep = mc.shape[0]
@@ -82,18 +87,18 @@
     pl.semaphore_wait(barrier, len(partners))
 
     def cols(qq, s):
-        return pl.ds(pl.multiple_of(qq * block + s * part, 128), part)
+        return pl.ds(pl.multiple_of(qq * block + sum(parts[:s]), 128), parts[s])
 
     def b_in(s, j):
-        return remote(weight.at[:, cols(peer(j), s)], b_v.at[s, dp],
+        return remote(weight.at[:, cols(peer(j), s)], b_v[s].at[dp],
                       bi_send.at[s, j], b_recv.at[s, dp], at(z, peer(j)))
 
     def b_own(s):
-        return pltpu.make_async_copy(weight.at[:, cols(q, s)], b_v.at[s, dp], bi_send.at[s, 0])
+        return pltpu.make_async_copy(weight.at[:, cols(q, s)], b_v[s].at[dp], bi_send.at[s, 0])
 
     def b_z(s, dpi, way, own=False):
-        src = weight.at[:, cols(q, s)] if own else b_v.at[s, dpi]
-        return remote(src, b_v.at[s, dpi], bz_send.at[way, s, dpi], b_recv.at[s, dpi],
+        src = weight.at[:, cols(q, s)] if own else b_v[s].at[dpi]
+        return remote(src, b_v[s].at[dpi], bz_send.at[way, s, dpi], b_recv.at[s, dpi],
                       at((z + (1 if way == 0 else layers - 1)) % layers, q))
 
     def b_send_z(s, dpi, way, own=False):
@@ -102,7 +107,7 @@
             b_z(s, dpi, way, own).start()
 
     def b_wait(s, dpi):
-        remote(b_v.at[s, dpi], b_v.at[s, dpi], bi_send.at[s, 0], b_recv.at[s, dpi], other).wait_recv()
+        remote(b_v[s].at[dpi], b_v[s].at[dpi], bi_send.at[s, 0], b_recv.at[s, dpi], other).wait_recv()
 
     def send_in(s):
         for j in range(1, SIDE):
@@ -163,6 +168,16 @@
         qq = peer(j)
         src = nxt if j == 0 else a_v.at[qq, c]
         return remote(src, a_v.at[qq, c], a_fwd.at[j], a_recv.at[qq, c], other)
+
+    def a_relay(h):
+        span = pl.ds(h * (half // 2), half // 2)
+        ref = a_v.at[peer(1 + h), c, :, span]
+        return remote(ref, ref, ar_send.at[h], ar_recv.at[h], at(z, peer(2 - h)))
+
+    def a_relay_wait(h):
+        span = pl.ds(h * (half // 2), half // 2)
+        ref = a_v.at[peer(3), c, :, span]
+        remote(ref, ref, ar_send.at[h], ar_recv.at[h], other).wait_recv()
 
     def a_wait(qq, cc):
         remote(a_v.at[qq, cc], a_v.at[qq, cc], a_send.at[0], a_recv.at[qq, cc], other).wait_recv()
@@ -248,10 +263,18 @@
         loop(width // wide, one)
         pltpu.make_async_copy(nw_v, new_weight, out_sem.at[1]).start()
 
+    def relay():
+        for h in range(2):
+            a_wait(peer(1 + h), c)
+            a_relay(h).start()
+            a_cross(1 + h).start()
+
+    def cross():
+        for h in range(2):
+            a_relay_wait(h)
+        a_cross(3).start()
+
     def tokens():
-        for j in range(1, SIDE):
-            a_wait(peer(j), c)
-            a_cross(j).start()
         loads[8].wait()
         for j in range(SIDE):
             a_wait(peer(j), 1 - c)
@@ -262,73 +285,116 @@
         loop(SIDE, one)
 
     def c_copy(s, m):
-        return remote(c_v.at[s, m], out.at[:, cols(q, s)], c_send.at[s, m], c_recv.at[s, q], at(z, m))
+        return remote(c_v[s].at[m], out.at[:, cols(q, s)], c_send.at[s, m], c_recv.at[s, q], at(z, m))
 
     def c_local(s):
-        return pltpu.make_async_copy(c_v.at[s, q], out.at[:, cols(q, s)], c_loc.at[s])
-
-    per = half // rows
+        return pltpu.make_async_copy(c_v[s].at[q], out.at[:, cols(q, s)], c_loc.at[s])
+
+    deep = SIDE * rows
+    fold = half // deep
+    final = jnp.where(z < layers // 2, layers - 1, 0)
+
+    def lay(m, k, s):
+        left = a_v[m, k // fold, :, pl.ds(pl.multiple_of((k % fold) * deep, 128), deep)]
+        right = b_v[s][pl.ds(k * SIDE, SIDE)].reshape(deep, parts[s])
+        return dot(left, right)
+
+    def low(m, s):
+        return dot(n_v[m], dirs[:, :, :, cols(q, s)].reshape(rank, parts[s]))
+
+    def leave(s, m, r):
+        c_v[s][m] = r.astype(BF)
+
+        @pl.when(m != q)
+        def _():
+            c_copy(s, m).start()
+
+        @pl.when(m == q)
+        def _():
+            c_local(s).start()
 
     def product(s):
         b_own(s).wait()
 
         def one(j):
-            m = peer((j + 1) % SIDE)
-            d = dirs[:, :, :, cols(q, s)].reshape(rank, part)
-            r = dot(n_v[m], d)
-            for cc in range(2):
-                r += dot(a_v[m, cc], b_v[s, cc * per:(cc + 1) * per].reshape(half, part))
-            c_v[s, m] = r.astype(BF)
-
-            @pl.when(m != q)
-            def _():
-                c_copy(s, m).start()
-
-            @pl.when(m == q)
-            def _():
-                c_local(s).start()
+            m = peer(SIDE - 1 - j)
+            r = low(m, s)
+            for k in range(layers):
+                r += lay(m, k, s)
+            leave(s, m, r)
         loop(SIDE, one)
 
-    send_own(0)
-    send_in(0)
-    gradient()
-    for j in range(1, SIDE):
-        a_copy(j).start()
-    a_cross(0).start()
-    for s in range(1, SPLITS):
-        send_in(s)
-    extra = [gradient_layer, adam, direction_layer, weights, tokens]
+    def product_start(s):
+        b_own(s).wait()
+
+        def one(m):
+            r = low(m, s)
+            for k in range(1, layers):
+                r += lay(m, (final + k) % layers, s)
+            acc_v[m] = r
+        loop(SIDE, one)
+
+    def product_end(s):
+        def one(j):
+            m = peer(SIDE - 1 - j)
+            leave(s, m, acc_v[m] + lay(m, final, s))
+        loop(SIDE, one)
+
     events = []
     for s in range(SPLITS):
         events.append((layers * s - s - 1.5, s, 0))
         for d in range(1, layers):
             events.append((layers * s - s + d, s, d))
+    events.sort()
+    last = len(events) - 1
+
+    def spread():
+        for j in range(1, 3):
+            a_copy(j).start()
+        a_cross(0).start()
+
+    steps = [
+        (PLACES[0], gradient_layer), (PLACES[1], adam), (PLACES[2], direction_layer),
+        (PLACES[3], relay), (PLACES[4], cross), (PLACES[5], weights), (PLACES[6], tokens),
+    ]
+    places = [(p * last // 15, step) for p, step in steps]
+    send_own(0)
+    send_in(0)
+    if EARLY:
+        send_own(1)
+    gradient()
+    send_in(1)
+    spread()
     ready = []
-    for _, s, d in sorted(events):
+    for i, (_, s, d) in enumerate(events):
+        if i == last:
+            for t in ready:
+                product(t)
+            product_start(s)
         if d == 0:
-            if s:
+            if s > EARLY:
                 send_own(s)
             layer_stage(s)
+            if 0 < s < SPLITS - 1:
+                send_in(s + 1)
         else:
             far_stage(s, d)
-        if d == layers - 1:
+        for p, step in places:
+            if p == i:
+                step()
+        if d == layers - 1 and i < last:
             ready.append(s)
-        if extra:
-            extra.pop(0)()
-        if not extra:
-            for t in ready:
-                product(t)
-            ready = []
-    while extra:
-        extra.pop(0)()
-    for t in ready:
-        product(t)
+        if i >= places[-1][0] and ready:
+            product(ready.pop(0))
+    product_end(SPLITS - 1)
 
     low_copy().wait_send()
     for j in range(1, SIDE):
         g_copy(j).wait_send()
         di_copy(j).wait_send()
-        a_copy(j).wait_send()
+    for j in range(2):
+        a_copy(1 + j).wait_send()
+        a_relay(j).wait_send()
     for j in range(SIDE):
         a_cross(j).wait_send()
     for o in range(1, layers):
@@ -355,7 +421,7 @@
     def done(j):
         qq = peer(j)
         for s in range(SPLITS):
-            remote(c_v.at[s, 0], out.at[:, cols(qq, s)], c_send.at[s, 0], c_recv.at[s, qq], other).wait_recv()
+            remote(c_v[s].at[0], out.at[:, cols(qq, s)], c_send.at[s, 0], c_recv.at[s, qq], other).wait_recv()
             c_copy(s, qq).wait_send()
     loop(SIDE, done, 1)
     for s in range(SPLITS):
@@ -366,7 +432,7 @@
     dp = lax.axis_size("dp")
     layers = dp // SIDE
     rows, width = weight.shape
-    part = width // SIDE // SPLITS
+    parts = [width // SIDE // UNITS * k for k in SHARES]
     tok, half = next_acts.shape
     rank = projection.shape[1]
     rstep = rank // dp
@@ -395,12 +461,13 @@
             pltpu.VMEM((rstep, width), F32),
             pltpu.VMEM((rows, width), BF),
             pltpu.VMEM((SIDE, 2, tok, half), BF),
-            pltpu.VMEM((SPLITS, dp, rows, part), BF),
+            [pltpu.VMEM((dp, rows, part), BF) for part in parts],
             pltpu.VMEM((SIDE, tok, rank), BF),
-            pltpu.VMEM((SPLITS, SIDE, tok, part), BF),
+            [pltpu.VMEM((SIDE, tok, part), BF) for part in parts],
+            pltpu.VMEM((SIDE, tok, parts[-1]), F32),
             dma(9), pltpu.SemaphoreType.DMA, pltpu.SemaphoreType.DMA, dma(SIDE), dma(SIDE),
             dma(layers), dma(layers),
-            dma(layers), dma(layers), dma(SIDE), dma(SIDE), dma(SIDE), dma(SIDE), dma(SIDE, 2),
+            dma(layers), dma(layers), dma(SIDE), dma(SIDE), dma(SIDE), dma(SIDE), dma(SIDE, 2), dma(2), dma(2),
             dma(SPLITS, SIDE), dma(2, SPLITS, dp), dma(SPLITS, dp),
             dma(SPLITS, SIDE), dma(SPLITS, SIDE), dma(SPLITS), dma(2),
         ],
@@ -427,11 +494,12 @@
         and dp % (2 * SIDE) == 0
         and rank % (16 * dp) == 0
         and weight.shape[0] % 16 == 0
-        and weight.shape[1] % (SIDE * SPLITS * 128) == 0
+        and weight.shape[1] % (SIDE * UNITS * 128) == 0
         and next_acts.shape[0] % 16 == 0
-        and next_acts.shape[1] % 128 == 0
+        and next_acts.shape[1] % 256 == 0
         and acts.shape[0] % 16 == 0
-        and next_acts.shape[1] % weight.shape[0] == 0
+        and next_acts.shape[1] % (SIDE * weight.shape[0]) == 0
+        and SIDE * weight.shape[0] % 128 == 0
     )
 
 

time: 322 us -> 208 us (0.65)
  Pallas kernels: 315 us -> 201 us
    pallas_call x1, Pallas kernels: 315 us -> 201 us  [fused(): pl.pallas_call(functools.partial(kernel, layers, acts.shape[0] * dp), out...]
where the time goes in v2:
time: 208 us
  Pallas kernels  201 us (97%)
  local copies, waits for them, and re-layouts  6.26 us (3%)
    pallas_call x1, Pallas kernels, fused(): pl.pallas_call(functools.partial(kernel, layers, acts.shape[0] * dp), out...  201 us
    unnamed x7, local copies, waits for them, and re-layouts  6.26 us

profile of v2, /device:TPU:0, one launch (start us, length us, event | category | flops | bytes accessed | tf_op | source)
XLA Modules:
  0.0 208.0 jit_solution(16411956002818851929)
XLA Ops:
  0.6 201.1 %shard_map.112 = (bf16[384,4096]{1,0:T(8,128)(2,1)}, bf16[320,4096]{1,0:T(8,128)(2,1)}, f32[16,4096]{1,0:T(8,128)}) custom-call(bf16[384,2560]{1,0:T(8,128)(2,1)} %acts.1, bf16[384,4096]{1,0:T(8,128)(2,1)} %grads.1, bf16[5120,256]{1,0:T(8,128)(2,1)} %proj.1, bf16[320,4096]{1,0:T(8,128)(2,1)} %weight.1, s32[16,4096]{1,0:T(8,128)} %mc.1, s32[16,128]{1,0:T(8,128)} %me.1, ...), custom_call_target="tpu_custom_call" | custom-call | tf_op jit(solution)/shard_map/pallas_call | solution.py:442
  201.7 0.0 copy-start
  201.7 4.1 %copy.15 = bf16[384,4096]{1,0:T(8,128)(2,1)} copy(bf16[384,4096]{1,0:T(8,128)(2,1)} %get-tuple-element.6) | data formatting | bytes 6291456
  205.8 0.0 copy-done
  205.8 0.0 copy-start.1
  205.8 1.5 copy.16
  207.3 0.0 copy-done.1
  207.3 0.7 copy.17
Async XLA Ops:
  201.7 4.1 %copy-start = (bf16[320,4096]{1,0:T(8,128)(2,1)S(1)}, bf16[320,4096]{1,0:T(8,128)(2,1)}, u32[]{:S(2)}) copy-start(bf16[320,4096]{1,0:T(8,128)(2,1)} %get-tuple-element.7) | copy-start | bytes 7864324
  205.8 1.5 copy-start.1
